TPU v7x, 32 devices: a whole 2x2x4 slice. The times are simulated.
32 devices in a mesh: store: 4 (over z), scorer: 8 (over y, x, core).
Axes of the slice: x: 2, y: 2, z: 4, core: 2. Of those that a mesh axis runs over, the one named last changes fastest.
Arguments:
- store_rows: bfloat16 [65536, 256], P(('store', 'scorer')), may hold values from -11 to 11
- cluster_logsize: bfloat16 [65536], P(('store', 'scorer')), may hold values from 0 to 318
- cluster_home: int32 [65536], replicated, may hold values from 0 to 65535, as said below
- cluster_ids: int32 [256, 512], P(('store', 'scorer')), may hold values from 0 to 65535, as said below
- valid_count: int32 [256], P(('store', 'scorer')), may hold values from 64 to 512
- candidates: bfloat16 [256, 512, 256], P(('store', 'scorer')), may hold values from -11 to 11
- cand_count: int32 [256], P(('store', 'scorer')), may hold values from 0 to 512, as said below
- candidate_row: int32 [256, 512], P(('store', 'scorer')), may hold values from 0 to 16383, as said below
- query_proj: bfloat16 [256, 256], replicated, may hold values from -0.375 to 0.375
- key_proj: bfloat16 [256, 256], replicated, may hold values from -0.375 to 0.375
- value_proj: bfloat16 [256, 256], replicated, may hold values from -0.375 to 0.375
- out_proj: bfloat16 [256, 256], replicated, may hold values from -0.375 to 0.375
- mlp_first: bfloat16 [512, 512], replicated, may hold values from -0.25 to 0.25
- bias_first: float32 [512], replicated, may hold values from -3 to 3
- mlp_second: bfloat16 [512, 256], replicated, may hold values from -0.25 to 0.25
- bias_second: float32 [256], replicated, may hold values from -3 to 3
- score_proj: bfloat16 [256], replicated, may hold values from -0.375 to 0.375
Outputs:
- span_scores: float32 [65536], P(('store', 'scorer'))
Inputs may be any that keep to these rules, and one draw needn't show every extreme that they name: A permutation: cluster c is row cluster_home[c] of store_rows. `cluster_ids`: of the 4096 entries of one device's requests, exactly 128 name clusters whose rows lie on each device's rows of store_rows, valid slots or not. `cand_count`: the counts of the 8 devices of one store group sum to 16384; in every group one device has all its requests full. `candidate_row`: the valid candidates of a store group fill each of its 16384 rows once; rows c * 2048 to (c + 1) * 2048 - 1 form span c, held by the group's device of scorer index c. One device has at most 512 valid candidates in one span, and in every group one device has exactly 512 in each span. Padded slots hold 0.
All inputs are finite; a program needn't handle non-finite values.
Results may differ from a plain program's by a relative error of at most 0.0065.
Values may be sent and summed in bfloat16 or wider, within the bound.
No kernel may reach another device: no remote copies, remote signals or barrier semaphores. Data moves between devices by JAX's collectives and lax.ppermute only.
A program may use at most 128 MiB of HBM per device.

v0:
```python
import math

import jax
import jax.numpy as jnp
from jax import lax
from jax.sharding import PartitionSpec as P

HEADS = 4


def attend(cand_block, key_rows, key_sizes, key_count, query_proj, key_proj, value_proj, out_proj):
    batch_size, cand_slots, row_width = cand_block.shape
    cluster_slots = key_rows.shape[1]
    head_size = row_width // HEADS
    queries = jnp.dot(
        cand_block.reshape(-1, row_width), query_proj, preferred_element_type=jnp.float32
    ).astype(jnp.bfloat16)
    keys_all = jnp.dot(
        key_rows.reshape(-1, row_width), key_proj, preferred_element_type=jnp.float32
    ).astype(jnp.bfloat16)
    values_all = jnp.dot(
        key_rows.reshape(-1, row_width), value_proj, preferred_element_type=jnp.float32
    ).astype(jnp.bfloat16)
    queries = queries.reshape(batch_size, cand_slots, HEADS, head_size)
    keys_all = keys_all.reshape(batch_size, cluster_slots, HEADS, head_size)
    values_all = values_all.reshape(batch_size, cluster_slots, HEADS, head_size)
    logits = jnp.einsum("bchd,bkhd->bhck", queries, keys_all, preferred_element_type=jnp.float32)
    logits = logits * (1.0 / math.sqrt(head_size)) + key_sizes.astype(jnp.float32)[:, None, None, :]
    usable = jnp.arange(cluster_slots, dtype=jnp.int32)[None, :] < key_count[:, None]
    logits = jnp.where(usable[:, None, None, :], logits, -1e30)
    row_max = jnp.max(logits, axis=-1, keepdims=True)
    weights = jnp.exp(logits - row_max)
    probs = (weights / jnp.sum(weights, axis=-1, keepdims=True)).astype(jnp.bfloat16)
    context = jnp.einsum(
        "bhck,bkhd->bchd", probs, values_all, preferred_element_type=jnp.float32
    ).astype(jnp.bfloat16)
    context = context.reshape(batch_size * cand_slots, row_width)
    attended = jnp.dot(context, out_proj, preferred_element_type=jnp.float32).astype(jnp.bfloat16)
    return attended.reshape(batch_size, cand_slots, row_width)


def score_rows(features, mlp_first, bias_first, mlp_second, bias_second, score_proj):
    hidden_one = jnp.maximum(
        jnp.dot(features, mlp_first, preferred_element_type=jnp.float32) + bias_first, 0.0
    ).astype(jnp.bfloat16)
    hidden_two = jnp.maximum(
        jnp.dot(hidden_one, mlp_second, preferred_element_type=jnp.float32) + bias_second, 0.0
    ).astype(jnp.bfloat16)
    return jnp.dot(hidden_two, score_proj, preferred_element_type=jnp.float32)


def select_rows(wanted, table_rows, table_sizes):
    table_count = table_rows.shape[0]
    selector = (wanted[:, None] == jnp.arange(table_count, dtype=jnp.int32)[None, :]).astype(
        jnp.bfloat16
    )
    picked_rows = jnp.dot(selector, table_rows, preferred_element_type=jnp.float32).astype(
        jnp.bfloat16
    )
    picked_sizes = jnp.dot(selector, table_sizes[:, None], preferred_element_type=jnp.float32)[
        :, 0
    ].astype(jnp.bfloat16)
    return (picked_rows, picked_sizes)


def serve_lookup(wanted, store_rows, cluster_logsize):
    total = wanted.shape[0]
    piece = math.gcd(total, 1024)

    def one_piece(piece_index):
        part_ids = lax.dynamic_slice_in_dim(wanted, piece_index * piece, piece, 0)
        return select_rows(part_ids, store_rows, cluster_logsize)

    found_rows, found_sizes = lax.map(one_piece, jnp.arange(total // piece, dtype=jnp.int32))
    return (found_rows.reshape(total, store_rows.shape[1]), found_sizes.reshape(total))


def on_device(
    store_rows,
    cluster_logsize,
    cluster_home,
    cluster_ids,
    valid_count,
    candidates,
    cand_count,
    candidate_row,
    query_proj,
    key_proj,
    value_proj,
    out_proj,
    mlp_first,
    bias_first,
    mlp_second,
    bias_second,
    score_proj,
):
    device_count = lax.axis_size(("store", "scorer"))
    scorer_count = lax.axis_size("scorer")
    req_dev, cluster_slots = cluster_ids.shape
    rows_dev, row_width = store_rows.shape
    cand_slots = candidates.shape[1]
    per_pair = req_dev * cluster_slots // device_count
    slot_total = req_dev * cluster_slots
    global_row = cluster_home[cluster_ids.reshape(-1)]
    home_dev = global_row // rows_dev
    local_row = global_row - home_dev * rows_dev
    tile = math.gcd(slot_total, 128)
    tile_count = slot_total // tile
    dest_hot = (home_dev[:, None] == jnp.arange(device_count, dtype=jnp.int32)[None, :]).astype(
        jnp.bfloat16
    )
    dest_tiles = dest_hot.reshape(tile_count, tile, device_count)
    lower = (
        jnp.arange(tile, dtype=jnp.int32)[:, None] >= jnp.arange(tile, dtype=jnp.int32)[None, :]
    ).astype(jnp.bfloat16)
    within_tile = jnp.einsum("ij,bjd->bid", lower, dest_tiles, preferred_element_type=jnp.float32)
    tile_totals = within_tile[:, tile - 1, :]
    earlier = jnp.cumsum(tile_totals, axis=0) - tile_totals
    running = (within_tile + earlier[:, None, :]).reshape(slot_total, device_count)
    ranking = (jnp.sum(running * dest_hot.astype(jnp.float32), axis=1) - 1.0).astype(jnp.int32)
    send_pos = home_dev * per_pair + ranking
    asked_rows = (
        jnp.zeros((slot_total,), jnp.int32)
        .at[send_pos]
        .set(local_row)
        .reshape(device_count, per_pair)
    )
    asked_here = lax.all_to_all(
        asked_rows, ("store", "scorer"), split_axis=0, concat_axis=0, tiled=True
    )
    item_count = asked_here.shape[1]
    found_rows, found_sizes = serve_lookup(asked_here.reshape(-1), store_rows, cluster_logsize)
    got_rows = lax.all_to_all(
        found_rows.reshape(device_count, item_count, row_width),
        ("store", "scorer"),
        split_axis=0,
        concat_axis=0,
        tiled=True,
    )
    got_sizes = lax.all_to_all(
        found_sizes.reshape(device_count, item_count),
        ("store", "scorer"),
        split_axis=0,
        concat_axis=0,
        tiled=True,
    )
    arrived_rows = got_rows.reshape(slot_total, row_width)
    arrived_sizes = got_sizes.reshape(slot_total)
    block_size = math.gcd(req_dev, 2)

    def one_block(block_index):
        block_start = block_index * block_size
        cand_block = lax.dynamic_slice_in_dim(candidates, block_start, block_size, 0)
        wanted = lax.dynamic_slice_in_dim(
            send_pos, block_start * cluster_slots, block_size * cluster_slots, 0
        )
        block_rows, block_sizes = select_rows(wanted, arrived_rows, arrived_sizes)
        block_rows = block_rows.reshape(block_size, cluster_slots, row_width)
        block_sizes = block_sizes.reshape(block_size, cluster_slots)
        key_count = lax.dynamic_slice_in_dim(valid_count, block_start, block_size, 0)
        return attend(
            cand_block,
            block_rows,
            block_sizes,
            key_count,
            query_proj,
            key_proj,
            value_proj,
            out_proj,
        )

    attended = lax.map(one_block, jnp.arange(req_dev // block_size, dtype=jnp.int32)).reshape(
        req_dev, cand_slots, row_width
    )
    features = jnp.concatenate([candidates, attended], axis=-1).reshape(
        req_dev * cand_slots, 2 * row_width
    )
    span_live = req_dev * cand_slots // 2
    pair_cap = req_dev * cand_slots // scorer_count
    valid_mask = (jnp.arange(cand_slots, dtype=jnp.int32)[None, :] < cand_count[:, None]).reshape(
        -1
    )
    flat_rows = candidate_row.reshape(-1)
    target_dev = flat_rows // span_live
    span_pos = flat_rows - target_dev * span_live
    onehot = (
        (target_dev[:, None] == jnp.arange(scorer_count, dtype=jnp.int32)[None, :])
        & valid_mask[:, None]
    ).astype(jnp.int32)
    rank_span = jnp.sum(jnp.cumsum(onehot, axis=0) * onehot, axis=1) - 1
    send_slot = jnp.where(valid_mask, target_dev * pair_cap + rank_span, scorer_count * pair_cap)
    spots = (
        jnp.full((scorer_count * pair_cap,), span_live, jnp.int32)
        .at[send_slot]
        .set(span_pos, mode="drop")
    )
    spots = spots.reshape(scorer_count, pair_cap)
    cand_score = score_rows(features, mlp_first, bias_first, mlp_second, bias_second, score_proj)
    packed = (
        jnp.zeros((scorer_count * pair_cap,), jnp.float32)
        .at[send_slot]
        .set(cand_score, mode="drop")
    )
    arrived, arrived_spots = (
        lax.all_to_all(
            packed.reshape(scorer_count, pair_cap),
            "scorer",
            split_axis=0,
            concat_axis=0,
            tiled=True,
        ),
        lax.all_to_all(spots, "scorer", split_axis=0, concat_axis=0, tiled=True),
    )
    span_scores = (
        jnp.zeros((span_live,), jnp.float32)
        .at[arrived_spots.reshape(-1)]
        .set(arrived.reshape(-1), mode="drop")
    )
    return span_scores


def solution(mesh):
    in_specs = (
        P(("store", "scorer"), None),
        P(("store", "scorer")),
        P(),
        P(("store", "scorer"), None),
        P(("store", "scorer")),
        P(("store", "scorer"), None, None),
        P(("store", "scorer")),
        P(("store", "scorer"), None),
        P(),
        P(),
        P(),
        P(),
        P(),
        P(),
        P(),
        P(),
        P(),
    )
    out_specs = P(("store", "scorer"))
    return jax.shard_map(
        on_device, mesh=mesh, in_specs=in_specs, out_specs=out_specs, check_vma=False
    )
```

profile of v0, /device:TPU:0, one launch (start us, length us, event | category | flops | bytes accessed | tf_op | source)
XLA Modules:
  0.0 325.9 jit_solution(15027290076939480209)
XLA Ops:
  0.8 19.5 %gather_fusion = s32[4096]{0:T(1024)S(1)} fusion(s32[65536]{0:T(1024)} %param.23, s32[4096]{0:T(1024)S(1)} %broadcast_clamp_fusion), kind=kCustom, calls=%fused_computation | custom fusion | bytes 49152 | tf_op jit(solution)/shard_map/gather | solution.py:104
  22.2 16.1 %scatter_custom_fusion.1 = s32[4096]{0:T(1024)} fusion(s32[4096]{0:T(1024)S(1)} %bitcast.191, s32[4096]{0:T(1024)S(1)} %get-tuple-element.235, s32[]{:T(128)} %constant.123.clone.1), kind=kCustom, calls=%fused_computation.129 | custom fusion | bytes 16388 | tf_op jit(solution)/shard_map/scatter | solution.py:125
  38.3 7.3 %all-to-all-start.1 = ((s32[32,1,128]{2,1,0:T(1,128)}), s32[32,1,128]{2,1,0:T(1,128)S(1)}, u32[]{:S(2)}, u32[]{:S(2)}) async-start(s32[32,1,128]{2,1,0:T(1,128)} %bitcast.26), calls=%async_computation.1 | async-start | bytes 32768 | tf_op jit(solution)/shard_map/all_to_all | solution.py:128
  45.6 7.1 %all-to-all-done.1 = s32[32,1,128]{2,1,0:T(1,128)S(1)} async-done(((s32[32,1,128]{2,1,0:T(1,128)}), s32[32,1,128]{2,1,0:T(1,128)S(1)}, u32[]{:S(2)}, u32[]{:S(2)}) %all-to-all-start.1) | async-done | bytes 16416 | tf_op jit(solution)/shard_map/all_to_all | solution.py:128
  52.7 21.2 %while.24 = (s32[]{:T(128)}, bf16[4,1024,256]{2,1,0:T(8,128)(2,1)}, bf16[4,1024]{1,0:T(4,128)(2,1)S(1)}, s32[4]{0:T(128)S(1)}, s32[4096]{0:T(1024)S(1)}, /*index...) while((s32[]{:T(128)}, bf16[4,1024,256]{2,1,0:T(8,128)(2,1)}, ...), condition=%wide.region_8.9_spmd, body=%wide.region_7.8_spmd.sunk | while | flops 1082393600 | bytes 1620655 | solution.py:74
  54.0 2.3 fusion.111
  56.3 1.6 fusion.112
  59.3 2.3 fusion.111
  61.6 1.6 fusion.112
  64.6 2.3 fusion.111
  67.0 1.6 fusion.112
  70.0 2.3 fusion.111
  72.3 1.6 fusion.112
  74.1 9.0 %all_to_all.45 = bf16[32,1,128]{2,1,0:T(2,128)(2,1)S(1)} all-to-all(bf16[32,1,128]{2,1,0:T(2,128)(2,1)S(1)} %all_to_all.39), channel_id=1, replica_groups=mesh['store'=4,'scorer'=8] {'store','scorer'}, dimensions={0} | all-to-all | bytes 16384 | tf_op jit(solution)/shard_map/all_to_all | solution.py:140
  83.1 2.7 all-to-all-start.2
  86.7 2.3 reduce-window.6
  90.0 16.1 %scatter_custom_fusion = s32[4096]{0:T(1024)} fusion(s32[4096]{0:T(1024)S(1)} %bitcast.195, s32[4096]{0:T(1024)S(1)} %get-tuple-element.237, s32[]{:T(128)} %constant.121.clone.1), kind=kCustom, calls=%fused_computation.131 | custom fusion | bytes 16388 | tf_op jit(solution)/shard_map/scatter | solution.py:195
  106.1 28.6 %all-to-all-done.2 = bf16[32,128,256]{2,1,0:T(8,128)(2,1)S(1)} async-done(((bf16[32,128,256]{2,1,0:T(8,128)(2,1)}), bf16[32,128,256]{2,1,0:T(8,128)(2,1)S(1)}, u32[]{:S(2)}, u32[]{:S(2)}) %all-to-all-start.2) | async-done | bytes 2097184 | tf_op jit(solution)/shard_map/all_to_all | solution.py:133
  134.7 3.9 %all-to-all-start = ((s32[8,1,512]{2,1,0:T(1,128)}), s32[8,1,512]{2,1,0:T(1,128)}, u32[]{:S(2)}, u32[]{:S(2)}) async-start(s32[8,1,512]{2,1,0:T(1,128)} %bitcast.14), calls=%async_computation | async-start | bytes 32768 | tf_op jit(solution)/shard_map/all_to_all | solution.py:212
  138.7 135.4 %while.25 = (s32[]{:T(128)}, bf16[4,2,512,256]{3,2,1,0:T(8,128)(2,1)}, s32[4]{0:T(128)S(1)}, s32[4096]{0:T(1024)S(1)}, bf16[4096,256]{1,0:T(8,128)(2,1)S(1)}, /*...) while((s32[]{:T(128)}, ...), condition=%wide.region_12.13_spmd, body=%wide.region_9.12_spmd.sunk | while | flops 3260549632 | bytes 72056136 | solution.py:172
  140.3 2.8 fusion.127
  145.3 1.1 constant_dynamic-slice_fusion.2
  147.1 4.5 %fusion.128 = f32[2,4,512,512]{2,3,1,0:T(8,128)} fusion(bf16[2,512,4,64]{3,2,1,0:T(4,128)(2,1)S(1)} %reshape.557, bf16[2,512,4,64]{3,2,1,0:T(4,128)(2,1)S(1)} %reshape.558), kind=kOutput, calls=%fused_computation.37.clone.1 | convolution fusion | flops 268435456 | bytes 9437184 | tf_op jit(solution)/shard_map/while/body/eval_jaxpr/bchd,bkhd->bhck/dot_general | solution.py:27
  151.6 3.1 fusion.129
  154.9 10.9 %fusion.131 = (f32[2,4,512]{2,1,0:T(4,128)S(1)}, f32[2,4,512,512]{2,3,1,0:T(8,128)}) fusion(f32[2,4,512,512]{2,3,1,0:T(8,128)} %fusion.128, f32[2,512]{1,0:T(2,128)S(1)} %fusion.130, pred[2,512]{1,0:T(4,128)(4,1)S(1)} %iota_compare_fusion.28), kind=kOutput, calls=%fused_computation.137.clone.1 | output fusion | flops 16777728 | bytes 16798720 | tf_op jit(solution)/shard_map/while/body/eval_jaxpr/sub | solution.py:32
  166.5 4.3 %fusion.132 = bf16[2,512,4,64]{1,3,2,0:T(8,128)(2,1)S(1)} fusion(f32[2,4,512,512]{2,3,1,0:T(8,128)} %get-tuple-element.359, f32[2,4,512]{2,1,0:T(4,128)S(1)} %get-tuple-element.360, bf16[2,512,4,64]{3,2,1,0:T(4,128)(2,1)S(1)} %reshape.560), kind=kOutput, calls=%fused_computation.36.clone.1 | convolution fusion | flops 272891904 | bytes 9453568 | tf_op jit(solution)/shard_map/while/body/eval_jaxpr/bhck,bkhd->bchd/dot_general | solution.py:34
  174.1 2.9 fusion.127
  179.1 1.1 constant_dynamic-slice_fusion.2
  180.9 4.5 %fusion.128 = f32[2,4,512,512]{2,3,1,0:T(8,128)} fusion(bf16[2,512,4,64]{3,2,1,0:T(4,128)(2,1)S(1)} %reshape.557, bf16[2,512,4,64]{3,2,1,0:T(4,128)(2,1)S(1)} %reshape.558), kind=kOutput, calls=%fused_computation.37.clone.1 | convolution fusion | flops 268435456 | bytes 9437184 | tf_op jit(solution)/shard_map/while/body/eval_jaxpr/bchd,bkhd->bhck/dot_general | solution.py:27
  185.4 3.1 fusion.129
  188.7 10.9 %fusion.131 = (f32[2,4,512]{2,1,0:T(4,128)S(1)}, f32[2,4,512,512]{2,3,1,0:T(8,128)}) fusion(f32[2,4,512,512]{2,3,1,0:T(8,128)} %fusion.128, f32[2,512]{1,0:T(2,128)S(1)} %fusion.130, pred[2,512]{1,0:T(4,128)(4,1)S(1)} %iota_compare_fusion.28), kind=kOutput, calls=%fused_computation.137.clone.1 | output fusion | flops 16777728 | bytes 16798720 | tf_op jit(solution)/shard_map/while/body/eval_jaxpr/sub | solution.py:32
  200.3 4.3 %fusion.132 = bf16[2,512,4,64]{1,3,2,0:T(8,128)(2,1)S(1)} fusion(f32[2,4,512,512]{2,3,1,0:T(8,128)} %get-tuple-element.359, f32[2,4,512]{2,1,0:T(4,128)S(1)} %get-tuple-element.360, bf16[2,512,4,64]{3,2,1,0:T(4,128)(2,1)S(1)} %reshape.560), kind=kOutput, calls=%fused_computation.36.clone.1 | convolution fusion | flops 272891904 | bytes 9453568 | tf_op jit(solution)/shard_map/while/body/eval_jaxpr/bhck,bkhd->bchd/dot_general | solution.py:34
  207.9 2.9 fusion.127
  214.7 4.5 %fusion.128 = f32[2,4,512,512]{2,3,1,0:T(8,128)} fusion(bf16[2,512,4,64]{3,2,1,0:T(4,128)(2,1)S(1)} %reshape.557, bf16[2,512,4,64]{3,2,1,0:T(4,128)(2,1)S(1)} %reshape.558), kind=kOutput, calls=%fused_computation.37.clone.1 | convolution fusion | flops 268435456 | bytes 9437184 | tf_op jit(solution)/shard_map/while/body/eval_jaxpr/bchd,bkhd->bhck/dot_general | solution.py:27
  219.2 3.1 fusion.129
  222.5 10.9 %fusion.131 = (f32[2,4,512]{2,1,0:T(4,128)S(1)}, f32[2,4,512,512]{2,3,1,0:T(8,128)}) fusion(f32[2,4,512,512]{2,3,1,0:T(8,128)} %fusion.128, f32[2,512]{1,0:T(2,128)S(1)} %fusion.130, pred[2,512]{1,0:T(4,128)(4,1)S(1)} %iota_compare_fusion.28), kind=kOutput, calls=%fused_computation.137.clone.1 | output fusion | flops 16777728 | bytes 16798720 | tf_op jit(solution)/shard_map/while/body/eval_jaxpr/sub | solution.py:32
  234.1 4.3 %fusion.132 = bf16[2,512,4,64]{1,3,2,0:T(8,128)(2,1)S(1)} fusion(f32[2,4,512,512]{2,3,1,0:T(8,128)} %get-tuple-element.359, f32[2,4,512]{2,1,0:T(4,128)S(1)} %get-tuple-element.360, bf16[2,512,4,64]{3,2,1,0:T(4,128)(2,1)S(1)} %reshape.560), kind=kOutput, calls=%fused_computation.36.clone.1 | convolution fusion | flops 272891904 | bytes 9453568 | tf_op jit(solution)/shard_map/while/body/eval_jaxpr/bhck,bkhd->bchd/dot_general | solution.py:34
  241.6 2.9 fusion.127
  248.5 4.5 %fusion.128 = f32[2,4,512,512]{2,3,1,0:T(8,128)} fusion(bf16[2,512,4,64]{3,2,1,0:T(4,128)(2,1)S(1)} %reshape.557, bf16[2,512,4,64]{3,2,1,0:T(4,128)(2,1)S(1)} %reshape.558), kind=kOutput, calls=%fused_computation.37.clone.1 | convolution fusion | flops 268435456 | bytes 9437184 | tf_op jit(solution)/shard_map/while/body/eval_jaxpr/bchd,bkhd->bhck/dot_general | solution.py:27
  253.0 3.1 fusion.129
  256.3 10.9 %fusion.131 = (f32[2,4,512]{2,1,0:T(4,128)S(1)}, f32[2,4,512,512]{2,3,1,0:T(8,128)}) fusion(f32[2,4,512,512]{2,3,1,0:T(8,128)} %fusion.128, f32[2,512]{1,0:T(2,128)S(1)} %fusion.130, pred[2,512]{1,0:T(4,128)(4,1)S(1)} %iota_compare_fusion.28), kind=kOutput, calls=%fused_computation.137.clone.1 | output fusion | flops 16777728 | bytes 16798720 | tf_op jit(solution)/shard_map/while/body/eval_jaxpr/sub | solution.py:32
  267.9 4.3 %fusion.132 = bf16[2,512,4,64]{1,3,2,0:T(8,128)(2,1)S(1)} fusion(f32[2,4,512,512]{2,3,1,0:T(8,128)} %get-tuple-element.359, f32[2,4,512]{2,1,0:T(4,128)S(1)} %get-tuple-element.360, bf16[2,512,4,64]{3,2,1,0:T(4,128)(2,1)S(1)} %reshape.560), kind=kOutput, calls=%fused_computation.36.clone.1 | convolution fusion | flops 272891904 | bytes 9453568 | tf_op jit(solution)/shard_map/while/body/eval_jaxpr/bhck,bkhd->bchd/dot_general | solution.py:34
  274.1 6.6 %maximum_convert_fusion = bf16[4096,512]{1,0:T(8,128)(2,1)} fusion(bf16[512,512]{1,0:T(8,128)(2,1)S(1)} %copy-done, bf16[4096,256]{1,0:T(8,128)(2,1)} %bitcast.30, bf16[4096,256]{1,0:T(8,128)(2,1)} %bitcast.173, f32[512]{0:T(512)S(1)} %copy-done.17), kind=kOutput, calls=%fused_computation.48 | convolution fusion | flops 2162163712 | bytes 8914944 | tf_op jit(solution)/shard_map/dot_general | solution.py:44
  280.7 4.1 %fusion.35 = f32[1,4096]{1,0:T(1,128)S(1)} fusion(bf16[256,1]{0,1:T(2,128)(2,1)S(1)} %copy-done.21, bf16[4096,512]{1,0:T(8,128)(2,1)} %maximum_convert_fusion, bf16[512,256]{1,0:T(8,128)(2,1)S(1)} %copy-done.16, f32[256]{0:T(256)S(1)} %copy-done.18), kind=kOutput, calls=%fused_computation.55 | convolution fusion | flops 1078984704 | bytes 4474368 | tf_op jit(solution)/shard_map/dot_general | solution.py:49
  284.8 16.2 %scatter_custom_fusion.2 = f32[4096]{0:T(1024)} fusion(s32[4096]{0:T(1024)} %bitcast.196, f32[4096]{0:T(1024)S(1)} %bitcast.198, f32[]{:T(128)} %constant.120.clone.1), kind=kCustom, calls=%fused_computation.125 | custom fusion | bytes 16896 | tf_op jit(solution)/shard_map/scatter | solution.py:202
  301.0 4.1 %all-to-all-start.4 = ((f32[8,1,512]{2,1,0:T(1,128)}), f32[8,1,512]{2,1,0:T(1,128)S(1)}, u32[]{:S(2)}, u32[]{:S(2)}) async-start(f32[8,1,512]{2,1,0:T(1,128)} %bitcast.32), calls=%async_computation.4 | async-start | bytes 32768 | tf_op jit(solution)/shard_map/all_to_all | solution.py:205
  305.8 4.0 %all-to-all-done.4 = f32[8,1,512]{2,1,0:T(1,128)S(1)} async-done(((f32[8,1,512]{2,1,0:T(1,128)}), f32[8,1,512]{2,1,0:T(1,128)S(1)}, u32[]{:S(2)}, u32[]{:S(2)}) %all-to-all-start.4) | async-done | bytes 16416 | tf_op jit(solution)/shard_map/all_to_all | solution.py:205
  309.9 16.1 %scatter_custom_fusion.3 = f32[2048]{0:T(1024)} fusion(s32[4096]{0:T(1024)S(1)} %bitcast.194, f32[4096]{0:T(1024)S(1)} %bitcast.193, f32[]{:T(128)} %constant.120.clone.1), kind=kCustom, calls=%fused_computation.133 | custom fusion | bytes 8196 | tf_op jit(solution)/shard_map/scatter | solution.py:217
  (246 shorter events, 32.7 us)
Async XLA Ops:
  0.0 274.1 %copy-start = (bf16[512,512]{1,0:T(8,128)(2,1)S(1)}, bf16[512,512]{1,0:T(8,128)(2,1)}, u32[]{:S(2)}) copy-start(bf16[512,512]{1,0:T(8,128)(2,1)} %param.33) | copy-start | bytes 1572868
  20.4 32.4 %copy-start.10 = (bf16[2048]{0:T(1024)(128)(2,1)S(1)}, bf16[2048]{0:T(1024)(128)(2,1)}, u32[]{:S(2)}) copy-start(bf16[2048]{0:T(1024)(128)(2,1)} %param.22) | copy-start | bytes 12292
  20.4 32.4 %copy-start.15 = (bf16[2048,256]{1,0:T(8,128)(2,1)S(1)}, bf16[2048,256]{1,0:T(8,128)(2,1)}, u32[]{:S(2)}) copy-start(bf16[2048,256]{1,0:T(8,128)(2,1)} %param.21) | copy-start | bytes 3145732
  38.3 14.4 %all-to-all-start.1 = ((s32[32,1,128]{2,1,0:T(1,128)}), s32[32,1,128]{2,1,0:T(1,128)S(1)}, u32[]{:S(2)}, u32[]{:S(2)}) async-start(s32[32,1,128]{2,1,0:T(1,128)} %bitcast.26), calls=%async_computation.1 | async-start | bytes 32768 | tf_op jit(solution)/shard_map/all_to_all | solution.py:128
  74.0 11.8 %copy-start.19 = (bf16[256]{0:T(256)(128)(2,1)S(1)}, bf16[256]{0:T(256)(128)(2,1)}, u32[]{:S(2)}) copy-start(bf16[256]{0:T(256)(128)(2,1)} %param.37) | copy-start | bytes 1540
  74.0 12.4 %copy-start.14 = (s32[8]{0:T(128)S(1)}, s32[8]{0:T(128)}, u32[]{:S(2)}) copy-start(s32[8]{0:T(128)} %param.27) | copy-start | bytes 100
  74.0 12.5 %copy-start.9 = (s32[8,512]{1,0:T(8,128)S(1)}, s32[8,512]{1,0:T(8,128)}, u32[]{:S(2)}) copy-start(s32[8,512]{1,0:T(8,128)} %param.28) | copy-start | bytes 49156
  74.0 64.6 %copy-start.3 = (bf16[256,256]{1,0:T(8,128)(2,1)S(1)}, bf16[256,256]{1,0:T(8,128)(2,1)}, u32[]{:S(2)}) copy-start(bf16[256,256]{1,0:T(8,128)(2,1)} %param.31) | copy-start | bytes 393220
  74.0 64.6 %copy-start.4 = (bf16[256,256]{1,0:T(8,128)(2,1)S(1)}, bf16[256,256]{1,0:T(8,128)(2,1)}, u32[]{:S(2)}) copy-start(bf16[256,256]{1,0:T(8,128)(2,1)} %param.29) | copy-start | bytes 393220
  74.1 64.6 %copy-start.5 = (bf16[256,256]{1,0:T(8,128)(2,1)S(1)}, bf16[256,256]{1,0:T(8,128)(2,1)}, u32[]{:S(2)}) copy-start(bf16[256,256]{1,0:T(8,128)(2,1)} %param.30) | copy-start | bytes 393220
  83.1 51.7 %all-to-all-start.2 = ((bf16[32,128,256]{2,1,0:T(8,128)(2,1)}), bf16[32,128,256]{2,1,0:T(8,128)(2,1)S(1)}, u32[]{:S(2)}, u32[]{:S(2)}) async-start(bf16[32,128,256]{2,1,0:T(8,128)(2,1)} %bitcast.175), calls=%async_computation.2 | async-start | bytes 4194304 | tf_op jit(solution)/shard_map/all_to_all | solution.py:133
  90.0 48.7 %copy-start.13 = (s32[4096,1]{0,1:T(1,128)}, s32[4096,1]{0,1:T(1,128)S(1)}, u32[]{:S(2)}) copy-start(s32[4096,1]{0,1:T(1,128)S(1)} %compare_select_fusion.3) | copy-start | bytes 49156
  134.7 166.3 %all-to-all-start = ((s32[8,1,512]{2,1,0:T(1,128)}), s32[8,1,512]{2,1,0:T(1,128)}, u32[]{:S(2)}, u32[]{:S(2)}) async-start(s32[8,1,512]{2,1,0:T(1,128)} %bitcast.14), calls=%async_computation | async-start | bytes 32768 | tf_op jit(solution)/shard_map/all_to_all | solution.py:212
  138.7 135.4 %copy-start.17 = (f32[512]{0:T(512)S(1)}, f32[512]{0:T(512)}, u32[]{:S(2)}) copy-start(f32[512]{0:T(512)} %param.34) | copy-start | bytes 6148
  138.9 4.2 %copy-start.7 = (bf16[4096,256]{1,0:T(8,128)(2,1)}, bf16[4096,256]{1,0:T(8,128)(2,1)S(1)}, u32[]{:S(2)}) copy-start(bf16[4096,256]{1,0:T(8,128)(2,1)S(1)} %get-tuple-element.434) | copy-start | bytes 6291460 | tf_op jit(solution)/shard_map/while
  138.9 4.2 %copy-start.11 = (s32[4096]{0:T(1024)}, s32[4096]{0:T(1024)S(1)}, u32[]{:S(2)}) copy-start(s32[4096]{0:T(1024)S(1)} %get-tuple-element.433) | copy-start | bytes 49156 | tf_op jit(solution)/shard_map/while
  138.9 4.2 %copy-start.22 = (s32[4]{0:T(128)}, s32[4]{0:T(128)S(1)}, u32[]{:S(2)}) copy-start(s32[4]{0:T(128)S(1)} %get-tuple-element.432) | copy-start | bytes 52 | tf_op jit(solution)/shard_map/while
  151.6 3.2 copy-start.20
  154.9 10.9 %copy-start.2 = (bf16[1024,256]{1,0:T(8,128)(2,1)S(1)}, bf16[1024,256]{1,0:T(8,128)(2,1)}, u32[]{:S(2)}) copy-start(bf16[1024,256]{1,0:T(8,128)(2,1)} %copy-done.1) | copy-start | bytes 1572868 | tf_op jit(solution)/shard_map/while
  166.5 5.0 %copy-start.6 = (bf16[256,256]{1,0:T(8,128)(2,1)S(1)}, bf16[256,256]{1,0:T(8,128)(2,1)}, u32[]{:S(2)}) copy-start(bf16[256,256]{1,0:T(8,128)(2,1)} %get-tuple-element.441) | copy-start | bytes 393220 | tf_op jit(solution)/shard_map/while
  170.8 1.9 copy-start.8
  170.8 1.9 copy-start.12
  172.7 4.2 %copy-start.7 = (bf16[4096,256]{1,0:T(8,128)(2,1)}, bf16[4096,256]{1,0:T(8,128)(2,1)S(1)}, u32[]{:S(2)}) copy-start(bf16[4096,256]{1,0:T(8,128)(2,1)S(1)} %get-tuple-element.434) | copy-start | bytes 6291460 | tf_op jit(solution)/shard_map/while
  172.7 4.2 %copy-start.11 = (s32[4096]{0:T(1024)}, s32[4096]{0:T(1024)S(1)}, u32[]{:S(2)}) copy-start(s32[4096]{0:T(1024)S(1)} %get-tuple-element.433) | copy-start | bytes 49156 | tf_op jit(solution)/shard_map/while
  172.7 4.2 %copy-start.22 = (s32[4]{0:T(128)}, s32[4]{0:T(128)S(1)}, u32[]{:S(2)}) copy-start(s32[4]{0:T(128)S(1)} %get-tuple-element.432) | copy-start | bytes 52 | tf_op jit(solution)/shard_map/while
  185.4 3.2 copy-start.20
  188.7 10.9 %copy-start.2 = (bf16[1024,256]{1,0:T(8,128)(2,1)S(1)}, bf16[1024,256]{1,0:T(8,128)(2,1)}, u32[]{:S(2)}) copy-start(bf16[1024,256]{1,0:T(8,128)(2,1)} %copy-done.1) | copy-start | bytes 1572868 | tf_op jit(solution)/shard_map/while
  200.3 5.0 %copy-start.6 = (bf16[256,256]{1,0:T(8,128)(2,1)S(1)}, bf16[256,256]{1,0:T(8,128)(2,1)}, u32[]{:S(2)}) copy-start(bf16[256,256]{1,0:T(8,128)(2,1)} %get-tuple-element.441) | copy-start | bytes 393220 | tf_op jit(solution)/shard_map/while
  204.6 1.9 copy-start.8
  204.6 1.9 copy-start.12
  204.6 1.9 copy-start.23
  206.5 4.2 %copy-start.7 = (bf16[4096,256]{1,0:T(8,128)(2,1)}, bf16[4096,256]{1,0:T(8,128)(2,1)S(1)}, u32[]{:S(2)}) copy-start(bf16[4096,256]{1,0:T(8,128)(2,1)S(1)} %get-tuple-element.434) | copy-start | bytes 6291460 | tf_op jit(solution)/shard_map/while
  206.5 4.2 %copy-start.11 = (s32[4096]{0:T(1024)}, s32[4096]{0:T(1024)S(1)}, u32[]{:S(2)}) copy-start(s32[4096]{0:T(1024)S(1)} %get-tuple-element.433) | copy-start | bytes 49156 | tf_op jit(solution)/shard_map/while
  206.5 4.2 %copy-start.22 = (s32[4]{0:T(128)}, s32[4]{0:T(128)S(1)}, u32[]{:S(2)}) copy-start(s32[4]{0:T(128)S(1)} %get-tuple-element.432) | copy-start | bytes 52 | tf_op jit(solution)/shard_map/while
  219.1 3.2 copy-start.20
  222.5 10.9 %copy-start.2 = (bf16[1024,256]{1,0:T(8,128)(2,1)S(1)}, bf16[1024,256]{1,0:T(8,128)(2,1)}, u32[]{:S(2)}) copy-start(bf16[1024,256]{1,0:T(8,128)(2,1)} %copy-done.1) | copy-start | bytes 1572868 | tf_op jit(solution)/shard_map/while
  234.1 5.0 %copy-start.6 = (bf16[256,256]{1,0:T(8,128)(2,1)S(1)}, bf16[256,256]{1,0:T(8,128)(2,1)}, u32[]{:S(2)}) copy-start(bf16[256,256]{1,0:T(8,128)(2,1)} %get-tuple-element.441) | copy-start | bytes 393220 | tf_op jit(solution)/shard_map/while
  238.4 1.9 copy-start.8
  240.3 4.2 %copy-start.7 = (bf16[4096,256]{1,0:T(8,128)(2,1)}, bf16[4096,256]{1,0:T(8,128)(2,1)S(1)}, u32[]{:S(2)}) copy-start(bf16[4096,256]{1,0:T(8,128)(2,1)S(1)} %get-tuple-element.434) | copy-start | bytes 6291460 | tf_op jit(solution)/shard_map/while
  240.3 4.2 %copy-start.11 = (s32[4096]{0:T(1024)}, s32[4096]{0:T(1024)S(1)}, u32[]{:S(2)}) copy-start(s32[4096]{0:T(1024)S(1)} %get-tuple-element.433) | copy-start | bytes 49156 | tf_op jit(solution)/shard_map/while
  240.3 4.2 %copy-start.22 = (s32[4]{0:T(128)}, s32[4]{0:T(128)S(1)}, u32[]{:S(2)}) copy-start(s32[4]{0:T(128)S(1)} %get-tuple-element.432) | copy-start | bytes 52 | tf_op jit(solution)/shard_map/while
  252.9 3.2 copy-start.20
  256.3 10.9 %copy-start.2 = (bf16[1024,256]{1,0:T(8,128)(2,1)S(1)}, bf16[1024,256]{1,0:T(8,128)(2,1)}, u32[]{:S(2)}) copy-start(bf16[1024,256]{1,0:T(8,128)(2,1)} %copy-done.1) | copy-start | bytes 1572868 | tf_op jit(solution)/shard_map/while
  267.9 5.0 %copy-start.6 = (bf16[256,256]{1,0:T(8,128)(2,1)S(1)}, bf16[256,256]{1,0:T(8,128)(2,1)}, u32[]{:S(2)}) copy-start(bf16[256,256]{1,0:T(8,128)(2,1)} %get-tuple-element.441) | copy-start | bytes 393220 | tf_op jit(solution)/shard_map/while
  274.1 6.6 %copy-start.16 = (bf16[512,256]{1,0:T(8,128)(2,1)S(1)}, bf16[512,256]{1,0:T(8,128)(2,1)}, u32[]{:S(2)}) copy-start(bf16[512,256]{1,0:T(8,128)(2,1)} %param.35) | copy-start | bytes 786436
  274.1 6.6 %copy-start.18 = (f32[256]{0:T(256)S(1)}, f32[256]{0:T(256)}, u32[]{:S(2)}) copy-start(f32[256]{0:T(256)} %param.36) | copy-start | bytes 3076
  274.1 6.6 %copy-start.21 = (bf16[256,1]{0,1:T(2,128)(2,1)S(1)}, bf16[256,1]{0,1:T(2,128)(2,1)}, u32[]{:S(2)}) copy-start(bf16[256,1]{0,1:T(2,128)(2,1)} %reshape.536) | copy-start | bytes 1540
  301.0 8.8 %all-to-all-start.4 = ((f32[8,1,512]{2,1,0:T(1,128)}), f32[8,1,512]{2,1,0:T(1,128)S(1)}, u32[]{:S(2)}, u32[]{:S(2)}) async-start(f32[8,1,512]{2,1,0:T(1,128)} %bitcast.32), calls=%async_computation.4 | async-start | bytes 32768 | tf_op jit(solution)/shard_map/all_to_all | solution.py:205
  (10 other events, 14.2 us)
where the time goes:
time: 327 us; the launch traced here: 326 us
  local copies, waits for them, and re-layouts  111 us (34%)
  matrix products  90.6 us (28%)
  other arithmetic  48.6 us (15%)
  waiting for transfers between devices  39.8 us (12%)
  starting transfers between devices  18 us (6%)
  blocking collectives  8.98 us (3%)
  loops' own time  8.59 us (3%)
    sub x4, other arithmetic, attend(): weights = jnp.exp(logits - row_max)  43.6 us
    all_to_all x1, waiting for transfers between devices, on_device(): lax.all_to_all(found_rows.reshape(device_count, item_count, row_width), (...  28.6 us
    dot_general x8, matrix products, select_rows(): jnp.dot(selector, table_rows, preferred_element_type=jnp.float32)  20.6 us
    gather x1, local copies, waits for them, and re-layouts, on_device(): global_row = cluster_home[cluster_ids.reshape(-1)]  19.5 us
    dot_general x8, matrix products, select_rows(): jnp.dot(selector, table_sizes[:, None], preferred_element_type=jnp.float32)  19 us
    dot_general x4, matrix products, attend(): jnp.einsum('bchd,bkhd->bhck', queries, keys_all, preferred_element_type=j...  17.9 us
    dot_general x4, matrix products, attend(): jnp.einsum('bhck,bkhd->bchd', probs, values_all, preferred_element_type=j...  17.2 us
    scatter x1, local copies, waits for them, and re-layouts, on_device(): packed = jnp.zeros((scorer_count * pair_cap,), jnp.float32).at[send_slot]...  16.2 us
  transfers between devices with their start and end apart: 4, of which 3 were waited for; matrix products, arithmetic and copies ran while one was open for 53% of the time, Pallas kernels for 0%

commit v1 on v0

v1 whole, which is shorter than its diff:
```python
import functools
import math

import jax
import jax.numpy as jnp
from jax import lax
from jax.experimental import pallas as pl
from jax.experimental.pallas import tpu as pltpu
from jax.sharding import PartitionSpec as P

HEADS = 4
LANES = 128
BLOCK = 16
DEAD = -1e30
HIGH = 65536
VMEM_LIMIT = 40 * 1024 * 1024


def dot(a, b):
    return jnp.dot(a, b, preferred_element_type=jnp.float32)


def dot_nt(a, b):
    return lax.dot_general(a, b, (((1,), (1,)), ((), ())), preferred_element_type=jnp.float32)


def hot(mask):
    return jnp.where(mask, 1.0, 0.0).astype(jnp.bfloat16)


def iota(shape, axis):
    return lax.broadcasted_iota(jnp.int32, shape, axis)


def whole(memory_space=pltpu.VMEM):
    return pl.BlockSpec(memory_space=memory_space)


def look_up(table_t, index, pieces):
    highs = table_t.shape[1]
    count = index.shape[1]
    rows = dot(table_t, hot(iota((highs, count), 0) == (index >> 7)))
    mine = iota((LANES, count), 0) == (index & (LANES - 1))
    found = jnp.zeros((1, count), jnp.float32)
    for piece in range(pieces):
        part = rows[piece * LANES : (piece + 1) * LANES]
        found = found + float(256**piece) * jnp.sum(
            jnp.where(mine, part, 0.0), axis=0, keepdims=True
        )
    return found


def ask_kernel(
    valid_ref, count_ref, ids_ref, home_ref, asked_ref, rank_ref, span_ref, table_ref, *, rows_dev
):
    requests, slots = ids_ref.shape
    devices, per_pair = asked_ref.shape
    pieces = table_ref.shape[0] // LANES
    for piece in range(pieces):
        part = (home_ref[...] >> (8 * piece)) & 255
        table_ref[piece * LANES : (piece + 1) * LANES, :] = jnp.transpose(
            part.astype(jnp.float32)
        ).astype(jnp.bfloat16)
    table = table_ref[...]
    upto = hot(iota((slots, slots), 0) <= iota((slots, slots), 1))
    carry = jnp.zeros((devices, 1), jnp.float32)
    asked = jnp.zeros((devices, 2 * per_pair), jnp.float32)
    for r in range(requests):
        row = look_up(table, ids_ref[r : r + 1, :], pieces).astype(jnp.int32)
        dev = row // rows_dev
        local = row - dev * rows_dev
        live = iota((1, slots), 1) < jnp.where(count_ref[r] > 0, valid_ref[r], 0)
        dest = jnp.where((iota((devices, slots), 0) == dev) & live, 1.0, 0.0)
        running = dot(dest.astype(jnp.bfloat16), upto) + carry
        carry = running[:, slots - 1 : slots]
        rank_f = jnp.sum(dest * running, axis=0, keepdims=True) - 1.0
        rank = rank_f.astype(jnp.int32)
        at_rank = iota((per_pair, slots), 0) == rank
        local_f = local.astype(jnp.float32)
        high_f = (local >> 8).astype(jnp.float32)
        low_f = local_f - 256.0 * high_f
        values = jnp.concatenate(
            [jnp.where(at_rank, low_f, 0.0), jnp.where(at_rank, high_f, 0.0)], axis=0
        )
        asked = asked + dot_nt(dest.astype(jnp.bfloat16), values.astype(jnp.bfloat16))
        rank_ref[r : r + 1, :] = jnp.where(live, dev * LANES + rank, -1)
        span_ref[r] = jnp.min(jnp.where(live, rank_f, 1e9)).astype(jnp.int32)
        span_ref[requests + r] = jnp.max(rank_f).astype(jnp.int32)
    most = jnp.max(carry, axis=0, keepdims=True)
    asked = asked[:, :per_pair] + 256.0 * asked[:, per_pair:] + HIGH * most
    asked_ref[...] = asked.astype(jnp.int32)


def ask(valid_count, cand_count, cluster_ids, home_table, devices, per_pair, rows_dev):
    requests, slots = cluster_ids.shape
    highs = home_table.shape[0]
    pieces = -(-(highs * LANES - 1).bit_length() // 8)
    return pl.pallas_call(
        functools.partial(ask_kernel, rows_dev=rows_dev),
        in_specs=[whole(pltpu.SMEM), whole(pltpu.SMEM), whole(), whole()],
        out_specs=[whole(), whole(), whole(pltpu.SMEM)],
        out_shape=[
            jax.ShapeDtypeStruct((devices, per_pair), jnp.int32),
            jax.ShapeDtypeStruct((requests, slots), jnp.int32),
            jax.ShapeDtypeStruct((2 * requests,), jnp.int32),
        ],
        scratch_shapes=[pltpu.VMEM((pieces * LANES, highs), jnp.bfloat16)],
        compiler_params=pltpu.CompilerParams(vmem_limit_bytes=VMEM_LIMIT),
        cost_estimate=pl.CostEstimate(
            flops=4_000_000_000, bytes_accessed=1_000_000, transcendentals=0
        ),
        name="ask",
    )(valid_count, cand_count, cluster_ids, home_table)


def serve_kernel(asked_ref, store_ref, size_ref, *refs, first, sized):
    out_refs, column_ref = refs[:-1], refs[-1]
    devices, per_pair = asked_ref.shape
    rows_dev, width = store_ref.shape
    places = max(out_ref.shape[1] for out_ref in out_refs)
    asked = asked_ref[...] & (HIGH - 1)
    column_ref[...] = jnp.zeros(column_ref.shape, jnp.int32)
    column_ref[1 : per_pair + 1, :] = jnp.transpose(asked.astype(jnp.float32)).astype(jnp.int32)
    group = math.gcd(devices, 1 << (384 // places).bit_length() - 1)
    store = store_ref[...]
    lanes = iota((places, rows_dev), 1)
    if sized:
        size_t = jnp.transpose(size_ref[...].astype(jnp.float32)).astype(jnp.bfloat16)
    for start in range(0, devices, group):
        picks = []
        for d in range(start, start + group):
            column = column_ref[first : first + places, d : d + 1]
            picks.append(hot(column == lanes))
        found = dot(jnp.concatenate(picks, axis=0), store).reshape(group, places, width)
        if sized:
            asked_of = [asked[d : d + 1, :] for d in range(start, start + group)]
            sizes = look_up(size_t, jnp.concatenate(asked_of, axis=1), 1)
            rest = jnp.zeros((1, width - per_pair), jnp.float32)
            for g in range(group):
                mine = sizes[:, g * per_pair : (g + 1) * per_pair]
                mine = jnp.concatenate([mine, rest], axis=1)
                top = jnp.where(iota((places, width), 0) == 0, mine, found[g])
                out_refs[0][start + g] = top.astype(jnp.bfloat16)
        else:
            found = found.astype(jnp.bfloat16)
            for out_ref in out_refs:
                out_ref[start : start + group] = found[:, : out_ref.shape[1], :]


def serve(asked_here, store_rows, size_table, first, place_counts, sized):
    devices, per_pair = asked_here.shape
    rows_dev, width = store_rows.shape
    places = max(place_counts)
    column_rows = max(first + places, -(-(per_pair + 1) // BLOCK) * BLOCK)
    return pl.pallas_call(
        functools.partial(serve_kernel, first=first, sized=sized),
        in_specs=[whole(), whole(), whole()],
        out_specs=[whole() for _ in place_counts],
        out_shape=[
            jax.ShapeDtypeStruct((devices, count, width), jnp.bfloat16) for count in place_counts
        ],
        scratch_shapes=[pltpu.VMEM((column_rows, devices), jnp.int32)],
        compiler_params=pltpu.CompilerParams(vmem_limit_bytes=VMEM_LIMIT),
        cost_estimate=pl.CostEstimate(
            flops=2 * devices * places * rows_dev * width,
            bytes_accessed=2 * (rows_dev + devices * sum(place_counts)) * width,
            transcendentals=0,
        ),
        name="serve",
    )(asked_here, store_rows, size_table)


def column_of(row):
    return jnp.transpose(jnp.broadcast_to(row, (LANES, row.shape[1])))


def score_kernel(*refs, bases, from_place, to_place):
    (valid_ref, count_ref, span_ref, cand_ref, rank_ref, target_ref) = refs[:6]
    arrived_refs = refs[6 : 6 + len(bases)]
    (
        query_ref,
        key_ref,
        value_ref,
        out_proj_ref,
        first_ref,
        bias_first_ref,
        second_ref,
        bias_second_ref,
        score_ref,
        before_ref,
        table_ref,
        rows_ref,
        keys_ref,
        values_ref,
        size_ref,
    ) = refs[6 + len(bases) :]
    requests, slots = rank_ref.shape
    devices = arrived_refs[0].shape[0]
    cands, width = cand_ref.shape[1:]
    head_size = width // HEADS
    r = pl.program_id(0)
    valid = valid_ref[r]
    count = count_ref[r]
    first_place = span_ref[r] + 1
    last_place = span_ref[requests + r] + 1
    low_block = first_place // BLOCK
    high_block = last_place // BLOCK
    mine = (count > 0) & (last_place >= from_place) & (last_place < to_place)
    cand_part = math.gcd(cands, 256)
    highs = table_ref.shape[0]
    to_exp2 = math.log2(math.e) / math.sqrt(head_size)

    @pl.when(r == 0)
    def _():
        table_ref[...] = before_ref[...]
        heads_of = arrived_refs[0][:, :BLOCK, :LANES].astype(jnp.float32)
        at_top = iota(heads_of.shape, 1) == 0
        sizes = jnp.sum(jnp.where(at_top, heads_of, 0.0), axis=1)
        size_ref[...] = jnp.transpose(sizes).astype(jnp.bfloat16)

    def run(n):
        spot = rank_ref[pl.ds(r, 1), :n]
        at = (spot & (LANES - 1)) + 1
        place = (at // BLOCK) * (devices * BLOCK) + (spot // LANES) * BLOCK + at % BLOCK
        place = column_of(jnp.where(spot >= 0, place, -1))
        offset = look_up(size_ref[...], spot, 1) * math.sqrt(head_size)
        offset = jnp.where(spot >= 0, offset, DEAD)
        rows_ref[:n, :] = jnp.zeros((n, width), jnp.float32)
        for arrived_ref, base in zip(arrived_refs, bases):
            block_rows = devices * BLOCK
            blocks = arrived_ref.shape[1] // BLOCK

            def add_block(j, carry):
                start = pl.multiple_of(j * BLOCK, BLOCK)
                block = arrived_ref[:, pl.ds(start, BLOCK), :].reshape(block_rows, width)
                rel = place - (j + base) * block_rows
                lanes = iota((n, LANES), 1)
                picks = [hot(rel == lanes + g * LANES) for g in range(block_rows // LANES)]
                rows_ref[:n, :] += dot(jnp.concatenate(picks, axis=1), block)
                return carry

            lax.fori_loop(
                jnp.clip(low_block - base, 0, blocks),
                jnp.clip(high_block + 1 - base, 0, blocks),
                add_block,
                0,
            )
        rows = rows_ref[:n, :].astype(jnp.bfloat16)
        keys = dot(rows, key_ref[...]).astype(jnp.bfloat16)
        values = dot(rows, value_ref[...]).astype(jnp.bfloat16)
        head_of = iota((n, width), 1) // head_size
        zero = jnp.zeros((n, width), jnp.bfloat16)
        for h in range(HEADS):
            keys_ref[h, :n, :] = jnp.where(head_of == h, keys, zero)
            values_ref[h, :n, :] = jnp.where(head_of == h, values, zero)

        def part(c, carry):
            start = pl.multiple_of(c * cand_part, cand_part)
            cand = cand_ref[0, pl.ds(start, cand_part), :]
            queries = dot(cand, query_ref[...]).astype(jnp.bfloat16)
            context = jnp.zeros((cand_part, width), jnp.float32)
            for h in range(HEADS):
                logits = dot_nt(queries, keys_ref[h, :n, :]) + offset
                top = jnp.max(logits, axis=1, keepdims=True)
                weights = jnp.exp2((logits - top) * to_exp2)
                probs = weights * (1.0 / jnp.sum(weights, axis=1, keepdims=True))
                context = context + dot(probs.astype(jnp.bfloat16), values_ref[h, :n, :])
            attended = dot(context.astype(jnp.bfloat16), out_proj_ref[...]).astype(jnp.bfloat16)
            hidden = (
                dot(cand, first_ref[:width, :])
                + dot(attended, first_ref[width:, :])
                + bias_first_ref[...]
            )
            hidden = jnp.maximum(hidden, 0.0).astype(jnp.bfloat16)
            hidden = dot(hidden, second_ref[...]) + bias_second_ref[...]
            hidden = jnp.maximum(hidden, 0.0).astype(jnp.bfloat16)
            scores = dot_nt(jnp.broadcast_to(score_ref[...], (8, hidden.shape[1])), hidden)[:1]
            target = target_ref[pl.ds(r, 1), pl.ds(start, cand_part)]
            counted = iota((1, cand_part), 1) + start < count
            high_hot = hot((iota((highs, cand_part), 0) == (target >> 7)) & counted)
            at_low = iota((LANES, cand_part), 0) == (target & (LANES - 1))
            left = scores
            for _ in range(3):
                piece = left.astype(jnp.bfloat16).astype(jnp.float32)
                left = left - piece
                table_ref[...] += dot_nt(
                    high_hot, jnp.where(at_low, piece, 0.0).astype(jnp.bfloat16)
                )
            return carry

        lax.fori_loop(0, (count + cand_part - 1) // cand_part, part, 0)

    step = max(LANES, slots // 2)
    for n in range(step, slots + 1, step):

        @pl.when(mine & (valid > n - step) & (valid <= n))
        def _():
            run(n)


def score(scalars, candidates, ranks, candidate_row, arrived, weights, before, places):
    requests, cands, width = candidates.shape
    slots = ranks.shape[1]
    devices = arrived[0].shape[0]
    full = lambda shape: pl.BlockSpec(shape, lambda r, *_: (0,) * len(shape))
    highs = before.shape[0]
    bases = (0, arrived[0].shape[1] // BLOCK)[: len(arrived)]
    operands = [ranks, candidate_row, *arrived, *weights, before]
    return pl.pallas_call(
        functools.partial(score_kernel, bases=bases, from_place=places[0], to_place=places[1]),
        grid_spec=pltpu.PrefetchScalarGridSpec(
            num_scalar_prefetch=3,
            grid=(requests,),
            in_specs=[pl.BlockSpec((1, cands, width), lambda r, *_: (r, 0, 0))]
            + [full(x.shape) for x in operands],
            out_specs=full((highs, LANES)),
            scratch_shapes=[
                pltpu.VMEM((slots, width), jnp.float32),
                pltpu.VMEM((HEADS, slots, width), jnp.bfloat16),
                pltpu.VMEM((HEADS, slots, width), jnp.bfloat16),
                pltpu.VMEM((LANES, devices), jnp.bfloat16),
            ],
        ),
        out_shape=jax.ShapeDtypeStruct((highs, LANES), jnp.float32),
        compiler_params=pltpu.CompilerParams(
            vmem_limit_bytes=VMEM_LIMIT, dimension_semantics=("arbitrary",)
        ),
        cost_estimate=pl.CostEstimate(
            flops=10_000_000_000, bytes_accessed=5_000_000, transcendentals=4_000_000
        ),
        name="score",
    )(*scalars, candidates, *operands)


def on_device(
    store_rows,
    cluster_logsize,
    cluster_home,
    cluster_ids,
    valid_count,
    candidates,
    cand_count,
    candidate_row,
    query_proj,
    key_proj,
    value_proj,
    out_proj,
    mlp_first,
    bias_first,
    mlp_second,
    bias_second,
    score_proj,
):
    axes = ("store", "scorer")
    devices = lax.axis_size(axes)
    scorers = lax.axis_size("scorer")
    requests, slots = cluster_ids.shape
    rows_dev, width = store_rows.shape
    cands = candidates.shape[1]
    per_pair = requests * slots // devices
    span_live = requests * cands // 2

    exchange = functools.partial(
        lax.all_to_all, axis_name=axes, split_axis=0, concat_axis=0, tiled=True
    )
    asked, ranks, span = ask(
        valid_count,
        cand_count,
        cluster_ids,
        cluster_home.reshape(-1, LANES),
        devices,
        per_pair,
        rows_dev,
    )
    asked_here = exchange(asked)
    early = per_pair // 2
    in_blocks = lambda places: -(-places // BLOCK) * BLOCK
    totals = sorted({in_blocks(3 * per_pair // 4), in_blocks(7 * per_pair // 8), in_blocks(per_pair + 1)})
    lookup = (asked_here, store_rows, cluster_logsize.reshape(-1, LANES))
    (early_here,) = serve(*lookup, 0, [early], True)
    late_here = serve(*lookup, early, [total - early for total in totals], False)
    needed = jnp.max(asked_here[:, 0] // HIGH) + 1
    early_rows = exchange(early_here)

    weights = (
        query_proj,
        key_proj,
        value_proj,
        out_proj,
        mlp_first,
        bias_first.reshape(1, -1),
        mlp_second,
        bias_second.reshape(1, -1),
        score_proj.reshape(1, -1),
    )
    table = jnp.zeros((scorers * span_live // LANES, LANES), jnp.float32)
    scalars = (valid_count, cand_count, span)
    shared = (scalars, candidates, ranks, candidate_row)

    def finish(late_here, early_rows):
        late_rows = exchange(late_here)
        done = score(*shared, (early_rows,), weights, table, (0, early))
        return score(
            *shared, (early_rows, late_rows), weights, done, (early, early + late_here.shape[1])
        )

    level = sum((needed > total).astype(jnp.int32) for total in totals[:-1])
    branches = [
        lambda late, rows, i=i: finish(late[i], rows) for i in range(len(totals))
    ]
    table = lax.switch(level, branches, tuple(late_here), early_rows)
    parts = lax.all_to_all(
        table.reshape(scorers, span_live // LANES, LANES),
        "scorer",
        split_axis=0,
        concat_axis=0,
        tiled=True,
    )
    return jnp.sum(parts, axis=0).reshape(span_live)


def solution(mesh):
    rows = P(("store", "scorer"))
    in_specs = (
        P(("store", "scorer"), None),
        rows,
        P(),
        P(("store", "scorer"), None),
        rows,
        P(("store", "scorer"), None, None),
        rows,
        P(("store", "scorer"), None),
    ) + (P(),) * 9
    return jax.shard_map(
        on_device, mesh=mesh, in_specs=in_specs, out_specs=rows, check_vma=False
    )
```

time: 327 us -> 121 us (0.37)
  the two profiles are of different devices: /device:TPU:0 before, /device:TPU:16 now
where the time goes in v1:
time: 121 us
  blocking collectives  51.2 us (42%)
  waiting for transfers between devices  28.7 us (24%)
  Pallas kernels  26.6 us (22%)
  starting transfers between devices  10.4 us (9%)
  local copies, waits for them, and re-layouts  1.86 us (2%)
  other arithmetic  1.26 us (1%)
    all_to_all x1, blocking collectives, on_device(): lax.all_to_all(table.reshape(scorers, span_live // LANES, LANES), 'scorer...  40.4 us
    all_to_all x1, waiting for transfers between devices, on_device(): early_rows = exchange(early_here)  18.1 us
    pallas_call x2, Pallas kernels, score(): pl.pallas_call(functools.partial(score_kernel, bases=bases, from_place=pl...  12.9 us
    all_to_all x1, blocking collectives, on_device(): asked_here = exchange(asked)  10.8 us
    all_to_all x1, waiting for transfers between devices, finish(): late_rows = exchange(late_here)  10.7 us
    pallas_call x2, Pallas kernels, serve(): pl.pallas_call(functools.partial(serve_kernel, first=first, sized=sized),...  8.31 us
    all_to_all x1, starting transfers between devices, finish(): late_rows = exchange(late_here)  5.58 us
    pallas_call x1, Pallas kernels, ask(): pl.pallas_call(functools.partial(ask_kernel, rows_dev=rows_dev), in_specs...  5.37 us
  transfers between devices with their start and end apart: 2, of which 2 were waited for; matrix products, arithmetic and copies ran while one was open for 1% of the time, Pallas kernels for 11%

profile of v1, /device:TPU:16, one launch (start us, length us, event | category | flops | bytes accessed | tf_op | source)
XLA Modules:
  0.0 121.1 jit_solution(13580740097799309191)
XLA Ops:
  0.0 0.0 copy-start.1
  0.0 0.9 copy-done.1
  1.0 0.0 copy-start.2
  1.0 0.7 copy-done.2
  1.7 0.0 copy-start
  1.7 0.0 copy-start.3
  1.7 5.4 %ask.1 = (s32[32,128]{1,0:T(8,128)S(1)}, s32[8,512]{1,0:T(8,128)S(1)}, s32[16]{0:T(128)S(1)}) custom-call(s32[8]{0:T(128)} %valid_ref.1, s32[8]{0:T(128)} %count_ref.1, s32[8,512]{1,0:T(8,128)S(1)} %copy-done.2, s32[512,128]{1,0:T(8,128)S(1)} %bitcast.14), custom_call_target="tpu_custom_call" | custom-call | flops 4000000000 | bytes 1000000 | tf_op jit(solution)/shard_map/ask/pallas_call | solution.py:98
  7.1 10.8 %all_to_all.33 = s32[32,1,128]{2,1,0:T(1,128)S(1)} all-to-all(s32[32,1,128]{2,1,0:T(1,128)S(1)} %bitcast.13), channel_id=1, replica_groups=mesh['store'=4,'scorer'=8] {'store','scorer'}, dimensions={0} | all-to-all | bytes 32768 | tf_op jit(solution)/shard_map/all_to_all | solution.py:375
  17.9 0.0 copy-done
  17.9 0.0 copy-done.3
  17.9 3.7 %serve.3 = bf16[32,64,256]{2,1,0:T(8,128)(2,1)} custom-call(s32[32,128]{1,0:T(8,128)S(1)} %bitcast.10, bf16[2048,256]{1,0:T(8,128)(2,1)S(1)} %copy-done, bf16[16,128]{1,0:T(8,128)(2,1)S(1)} %bitcast.15), custom_call_target="tpu_custom_call" | custom-call | flops 2147483648 | bytes 2097152 | tf_op jit(solution)/shard_map/serve/pallas_call | solution.py:155
  21.6 0.0 copy-start.13
  21.6 4.8 %all-to-all-start.4 = ((bf16[32,64,256]{2,1,0:T(8,128)(2,1)}), bf16[32,64,256]{2,1,0:T(8,128)(2,1)S(1)}, u32[]{:S(2)}, u32[]{:S(2)}) async-start(bf16[32,64,256]{2,1,0:T(8,128)(2,1)} %serve.3), calls=%async_computation.4 | async-start | bytes 2097152 | tf_op jit(solution)/shard_map/all_to_all | solution.py:383
  26.4 0.0 copy-done.13
  26.5 0.1 slice_reduce_fusion
  26.6 0.6 fusion
  27.9 0.0 copy-start.4
  27.9 0.0 copy-start.5
  27.9 0.0 copy-start.6
  27.9 0.0 copy-start.7
  27.9 0.0 copy-start.8
  27.9 0.0 copy-start.10
  28.0 0.0 copy-start.11
  28.0 0.0 copy-start.14
  28.0 0.0 copy-start.16
  28.0 4.6 %serve.2 = (bf16[32,32,256]{2,1,0:T(8,128)(2,1)}, bf16[32,48,256]{2,1,0:T(8,128)(2,1)}, bf16[32,80,256]{2,1,0:T(8,128)(2,1)}) custom-call(s32[32,128]{1,0:T(8,128)S(1)} %bitcast.12, bf16[2048,256]{1,0:T(8,128)(2,1)S(1)} %copy-done, bf16[16,128]{1,0:T(8,128)(2,1)S(1)} %bitcast.16), custom_call_target="tpu_custom_call" | custom-call | flops 2684354560 | bytes 3670016 | tf_op jit(solution)/shard_map/serve/pallas_call | solution.py:155
  32.6 18.1 %all-to-all-done.4 = bf16[32,64,256]{2,1,0:T(8,128)(2,1)S(1)} async-done(((bf16[32,64,256]{2,1,0:T(8,128)(2,1)}), bf16[32,64,256]{2,1,0:T(8,128)(2,1)S(1)}, u32[]{:S(2)}, u32[]{:S(2)}) %all-to-all-start.4) | async-done | bytes 1048608 | tf_op jit(solution)/shard_map/all_to_all | solution.py:383
  50.6 0.0 copy-done.4
  50.6 0.0 copy-done.5
  50.6 0.0 copy-done.6
  50.7 0.0 copy-done.7
  50.7 0.0 copy-done.8
  50.7 0.0 copy-done.10
  50.7 0.0 copy-done.11
  50.7 0.0 copy-done.14
  50.7 0.0 copy-done.16
  50.7 29.4 %conditional.1 = (f32[128,128]{1,0:T(8,128)S(1)}) conditional(s32[]{:T(128)} %clamp.3, (bf16[32,32,256]{2,1,0:T(8,128)(2,1)}, s32[8]{0:T(128)S(1)}, s32[8]{0:T(128)S(1)}, s32[16]{0:T(128)S(1)}, bf16[8,512,256]{2,1,0:T(8,128)(2,1)}, /*index=5*/s32[8,512]{1,0:T(8,128)S(1)}, s32[8,512]{1,0:T(8,128)S(1)}, ...), branch_computations={%region_1.2_spmd, %region_2.3_spmd, %region_3.4_spmd} | conditional | flops 20000000000 | bytes 14594416 | solution.py:411
  51.0 5.6 %all-to-all-start.1 = ((bf16[32,48,256]{2,1,0:T(8,128)(2,1)}), bf16[32,48,256]{2,1,0:T(8,128)(2,1)S(1)}, u32[]{:S(2)}, u32[]{:S(2)}) async-start(bf16[32,48,256]{2,1,0:T(8,128)(2,1)} %get-tuple-element.135), calls=%async_computation.1 | async-start | bytes 1572864 | tf_op jit(solution)/shard_map/cond/branch_1_fun/all_to_all | solution.py:401
  56.6 8.2 %score.8.refs_17_ = f32[128,128]{1,0:T(8,128)S(1)} custom-call(s32[8]{0:T(128)S(1)} %get-tuple-element.128.refs_0_, s32[8]{0:T(128)S(1)} %get-tuple-element.129.refs_1_, s32[16]{0:T(128)S(1)} %get-tuple-element.130.refs_2_, bf16[8,512,256]{2,1,0:T(8,128)(2,1)} %get-tuple-element.131.refs_3_, s32[8,512]{1,0:T(8,128)S(1)} %get-tuple-element.132.refs_4_, ...), custom_call_target="tpu_custom_call" | custom-call | flops 10000000000 | bytes 5000000 | tf_op jit(solution)/shard_map/cond/branch_1_fun/score/pallas_call | solution.py:309
  64.8 10.7 %all-to-all-done.1.refs_7_ = bf16[32,48,256]{2,1,0:T(8,128)(2,1)S(1)} async-done(((bf16[32,48,256]{2,1,0:T(8,128)(2,1)}), bf16[32,48,256]{2,1,0:T(8,128)(2,1)S(1)}, u32[]{:S(2)}, u32[]{:S(2)}) %all-to-all-start.1) | async-done | bytes 786464 | tf_op jit(solution)/shard_map/cond/branch_1_fun/all_to_all | solution.py:401
  75.4 4.7 %score.9 = f32[128,128]{1,0:T(8,128)S(1)} custom-call(s32[8]{0:T(128)S(1)} %get-tuple-element.128.refs_0_, s32[8]{0:T(128)S(1)} %get-tuple-element.129.refs_1_, s32[16]{0:T(128)S(1)} %get-tuple-element.130.refs_2_, bf16[8,512,256]{2,1,0:T(8,128)(2,1)} %get-tuple-element.131.refs_3_, s32[8,512]{1,0:T(8,128)S(1)} %get-tuple-element.132.refs_4_, ...), custom_call_target="tpu_custom_call" | custom-call | flops 10000000000 | bytes 5000000 | tf_op jit(solution)/shard_map/cond/branch_1_fun/score/pallas_call | solution.py:309
  80.1 40.4 %all_to_all.34 = f32[8,16,128]{2,1,0:T(8,128)S(1)} all-to-all(f32[8,16,128]{2,1,0:T(8,128)S(1)} %bitcast.17), channel_id=1, replica_groups=mesh['store'=4,'scorer'=8] {'scorer'}, dimensions={0} | all-to-all | bytes 131072 | tf_op jit(solution)/shard_map/all_to_all | solution.py:412
  120.5 0.6 reduce_sum.9
  (2 shorter events, 0.0 us)
Async XLA Ops:
  0.0 0.9 copy-start.1
  1.0 0.7 copy-start.2
  1.7 16.2 %copy-start = (bf16[2048,256]{1,0:T(8,128)(2,1)S(1)}, bf16[2048,256]{1,0:T(8,128)(2,1)}, u32[]{:S(2)}) copy-start(bf16[2048,256]{1,0:T(8,128)(2,1)} %store_ref.3) | copy-start | bytes 3145732
  1.7 16.2 %copy-start.3 = (bf16[2048]{0:T(1024)(128)(2,1)S(1)}, bf16[2048]{0:T(1024)(128)(2,1)}, u32[]{:S(2)}) copy-start(bf16[2048]{0:T(1024)(128)(2,1)} %param.21) | copy-start | bytes 12292
  21.6 4.8 %copy-start.13 = (bf16[256]{0:T(256)(128)(2,1)S(1)}, bf16[256]{0:T(256)(128)(2,1)}, u32[]{:S(2)}) copy-start(bf16[256]{0:T(256)(128)(2,1)} %param.36) | copy-start | bytes 1540
  21.6 29.0 %all-to-all-start.4 = ((bf16[32,64,256]{2,1,0:T(8,128)(2,1)}), bf16[32,64,256]{2,1,0:T(8,128)(2,1)S(1)}, u32[]{:S(2)}, u32[]{:S(2)}) async-start(bf16[32,64,256]{2,1,0:T(8,128)(2,1)} %serve.3), calls=%async_computation.4 | async-start | bytes 2097152 | tf_op jit(solution)/shard_map/all_to_all | solution.py:383
  27.9 22.8 %copy-start.4 = (bf16[512,512]{1,0:T(8,128)(2,1)S(1)}, bf16[512,512]{1,0:T(8,128)(2,1)}, u32[]{:S(2)}) copy-start(bf16[512,512]{1,0:T(8,128)(2,1)} %param.32) | copy-start | bytes 1572868
  27.9 22.8 %copy-start.5 = (bf16[512,256]{1,0:T(8,128)(2,1)S(1)}, bf16[512,256]{1,0:T(8,128)(2,1)}, u32[]{:S(2)}) copy-start(bf16[512,256]{1,0:T(8,128)(2,1)} %param.34) | copy-start | bytes 786436
  27.9 22.7 %copy-start.6 = (bf16[256,256]{1,0:T(8,128)(2,1)S(1)}, bf16[256,256]{1,0:T(8,128)(2,1)}, u32[]{:S(2)}) copy-start(bf16[256,256]{1,0:T(8,128)(2,1)} %param.28) | copy-start | bytes 393220
  27.9 22.7 %copy-start.7 = (bf16[256,256]{1,0:T(8,128)(2,1)S(1)}, bf16[256,256]{1,0:T(8,128)(2,1)}, u32[]{:S(2)}) copy-start(bf16[256,256]{1,0:T(8,128)(2,1)} %param.29) | copy-start | bytes 393220
  27.9 22.7 %copy-start.8 = (bf16[256,256]{1,0:T(8,128)(2,1)S(1)}, bf16[256,256]{1,0:T(8,128)(2,1)}, u32[]{:S(2)}) copy-start(bf16[256,256]{1,0:T(8,128)(2,1)} %param.30) | copy-start | bytes 393220
  27.9 22.7 %copy-start.10 = (s32[8,512]{1,0:T(8,128)S(1)}, s32[8,512]{1,0:T(8,128)}, u32[]{:S(2)}) copy-start(s32[8,512]{1,0:T(8,128)} %param.27) | copy-start | bytes 49156
  28.0 22.7 %copy-start.11 = (f32[256]{0:T(256)S(1)}, f32[256]{0:T(256)}, u32[]{:S(2)}) copy-start(f32[256]{0:T(256)} %param.35) | copy-start | bytes 3076
  28.0 22.7 %copy-start.14 = (s32[8]{0:T(128)S(1)}, s32[8]{0:T(128)}, u32[]{:S(2)}) copy-start(s32[8]{0:T(128)} %valid_ref.1) | copy-start | bytes 100
  28.0 22.7 %copy-start.16 = (s32[8]{0:T(128)S(1)}, s32[8]{0:T(128)}, u32[]{:S(2)}) copy-start(s32[8]{0:T(128)} %count_ref.1) | copy-start | bytes 100
  51.0 24.5 %all-to-all-start.1 = ((bf16[32,48,256]{2,1,0:T(8,128)(2,1)}), bf16[32,48,256]{2,1,0:T(8,128)(2,1)S(1)}, u32[]{:S(2)}, u32[]{:S(2)}) async-start(bf16[32,48,256]{2,1,0:T(8,128)(2,1)} %get-tuple-element.135), calls=%async_computation.1 | async-start | bytes 1572864 | tf_op jit(solution)/shard_map/cond/branch_1_fun/all_to_all | solution.py:401
